TPU v7x, 256 devices: a whole 4x4x8 slice. The times are simulated.
256 devices in a mesh: src: 32 (over x, y, core), tgt: 8 (over z).
Axes of the slice: x: 4, y: 4, z: 8, core: 2. Of those that a mesh axis runs over, the one named last changes fastest.
Arguments:
- sources: float32 [32768, 128], P(('src', 'tgt')), may hold values from -3 to 3
- targets: float32 [32768, 128], P(('tgt', 'src')), may hold values from -0.6 to 0.6
- log_src_mass: float32 [32768], P('src'), may hold values from -1 to 1
- log_tgt_mass: float32 [32768], P('tgt'), may hold values from -1 to 1
Outputs:
- src_potential: float32 [32768], P('src')
- tgt_potential: float32 [32768], P('tgt')
All inputs are finite; a program needn't handle non-finite values.
Results may differ from a plain program's by a relative error of at most 0.0003.
Values sent between devices are 32-bit elements; how exact they have to be, the bound alone decides.
No kernel may reach another device: no remote copies, remote signals or barrier semaphores. Data moves between devices by JAX's collectives and lax.ppermute only.
A program may use at most 64 MiB of HBM per device.

v0:
```python
import functools
import math

import jax
import jax.numpy as jnp
from jax import lax
from jax.experimental import pallas as pl
from jax.experimental.pallas import tpu as pltpu
from jax.sharding import Mesh
from jax.sharding import PartitionSpec as P

eps = 0.05
LOG2E = math.log2(math.e)
KAPPA = LOG2E / eps
SHIFT = 43.0
L = 128
B = 16
H = B // 2
N = B * L
F32 = jnp.float32
BF16 = jnp.bfloat16
VM = pl.BlockSpec(memory_space=pltpu.VMEM)
SM = pl.BlockSpec(memory_space=pltpu.SMEM)
VEC = (B, L)
NEAR = (0, 1, 7, 2, 6)
FAR = (3, 5, 4)
PARTS = ((0, 0), (0, 1), (1, 0), (1, 1), (0, 2), (2, 0))


def rows_of(q):
    return pl.ds(pl.multiple_of(q * L, L), L)


def lanes_of(s):
    return pl.ds(s * L, L)


def fold(x, op):
    return op(x.reshape(-1, 8, L), axis=0)


def spread(vec, out_ref):
    turned = jnp.concatenate([vec, jnp.zeros((L - B, L), F32)], axis=0).T
    for q in range(B):
        out_ref[q * L : (q + 1) * L, :] = jnp.broadcast_to(turned[:, q : q + 1], (L, L))


def split3(x):
    a = x.astype(BF16)
    x = x - a.astype(F32)
    b = x.astype(BF16)
    x = x - b.astype(F32)
    return a, b, x.astype(BF16)


def start_kernel(
    place_ref, near_ref, near_other_ref, far_ref, far_other_ref, tgt_ref, mass_ref, ls_other_ref,
    z_ref, pay_ref, sq_ref, ls_ref, s6, t6, beta,
):
    core, level = place_ref[0], place_ref[1]
    ls_ref[pl.ds(pl.multiple_of(core * H, H), H), :] = mass_ref[B:, :]
    ls_ref[pl.ds(pl.multiple_of((1 - core) * H, H), H), :] = ls_other_ref[...]
    for own, order, ref in (
        (True, NEAR, near_ref), (False, NEAR, near_other_ref), (True, FAR, far_ref), (False, FAR, far_other_ref),
    ):
        for at, step in enumerate(order):
            x = ref[at * L : (at + 1) * L, :]
            q = lax.rem(level + (H - step), H)
            if own:
                sq_ref[pl.ds(q, 1), :] = jnp.sum((x * x).T, axis=0, keepdims=True)
            parts = split3(x * (2.0 * KAPPA))
            rows = rows_of((core if own else 1 - core) * H + q)
            for c, (a, _) in enumerate(PARTS):
                s6[rows, c * L : (c + 1) * L] = parts[a]
    for q in range(B):
        t = tgt_ref[q * L : (q + 1) * L, :].T
        beta[q : q + 1, :] = LOG2E * mass_ref[q : q + 1, :] - KAPPA * jnp.sum(t * t, axis=0, keepdims=True)
        parts = split3(t)
        for c, (_, b) in enumerate(PARTS):
            t6[c * L : (c + 1) * L, q * L : (q + 1) * L] = parts[b]

    def product(rows, c):
        g = jnp.dot(s6[rows, :], t6[:, c * L : (c + 2) * L], preferred_element_type=F32)
        for s in range(2):
            z_ref[rows, lanes_of(c + s)] = g[:, s * L : (s + 1) * L] + beta[c + s : c + s + 1, :]

    def stats(q):
        rows = pl.ds(q * L, L)
        peak = z_ref[rows, lanes_of(0)]
        for s in range(1, B):
            peak = jnp.maximum(peak, z_ref[rows, lanes_of(s)])
        total = jnp.zeros((L, L), F32)
        for s in range(B):
            total = total + jnp.exp2(z_ref[rows, lanes_of(s)] - peak)
        peak = peak.T
        top = jnp.max(peak, axis=0, keepdims=True)
        pay_ref[q : q + 1, :] = top + jnp.log2(jnp.sum(total.T * jnp.exp2(peak - top), axis=0, keepdims=True))

    for half in range(3):
        for step in range(H):
            if half < 2:
                product(pl.ds(half * H * L, H * L), 2 * step)
            if half:
                stats((half - 1) * H + step)


def merge(got_ref):
    got = [got_ref[d] for d in range(B)]
    top = functools.reduce(jnp.maximum, got)
    return top + jnp.log2(functools.reduce(jnp.add, [jnp.exp2(x - top) for x in got]))


def add_up(got_ref):
    return functools.reduce(jnp.add, [got_ref[d] for d in range(B)])


def cols_kernel(z_ref, got_ref, ls_ref, e_ref, pay_ref, m_ref, alpha_ref, wide):
    alpha = LOG2E * ls_ref[...] - merge(got_ref)
    alpha_ref[...] = alpha
    spread(alpha, wide)

    def highest(q, peak):
        a = wide[rows_of(q), :]
        return tuple(jnp.maximum(peak[s], fold(z_ref[rows_of(q), lanes_of(s)] + a, jnp.max)) for s in range(B))

    peak = lax.fori_loop(0, B, highest, (jnp.full((8, L), -1e30, F32),) * B, unroll=2)
    for s in range(B):
        m_ref[s : s + 1, :] = jnp.max(peak[s], axis=0, keepdims=True)

    ahead = 3
    for c in range(0, B, H):

        def weigh(q, total, c=c):
            rows = pl.ds(pl.multiple_of(q * (L // 2), L // 2), L // 2)
            a = wide[rows, :] + SHIFT
            held = [z_ref[rows, lanes_of(c + s)] for s in range(ahead)]
            out = []
            for s in range(H):
                if s + ahead < H:
                    held.append(z_ref[rows, lanes_of(c + s + ahead)])
                e = jnp.exp2((held[s] + a) - m_ref[c + s : c + s + 1, :])
                e_ref[rows, lanes_of(c + s)] = e
                out.append(total[s] + fold(e, jnp.sum))
            return tuple(out)

        total = lax.fori_loop(0, 2 * B, weigh, (jnp.zeros((8, L), F32),) * H, unroll=2)
        for s in range(H):
            one = slice(c + s, c + s + 1)
            pay_ref[one, :] = m_ref[one, :] + (jnp.log2(jnp.sum(total[s], axis=0, keepdims=True)) - SHIFT)


def row_sums(e_ref, v_ref, pay_ref):
    def body(q, _):
        total = jnp.zeros((L, L), F32)
        for s in range(B):
            total = total + e_ref[rows_of(q), lanes_of(s)] * v_ref[s : s + 1, :]
        pay_ref[pl.ds(q, 1), :] = jnp.sum(total.T, axis=0, keepdims=True)
        return 0

    lax.fori_loop(0, B, body, 0, unroll=8)


def col_sums(e_ref, v0_ref, pay_ref, wide):
    def body(q, carry):
        u = wide[rows_of(q), :]
        return tuple(carry[s] + fold(e_ref[rows_of(q), lanes_of(s)] * u, jnp.sum) for s in range(B))

    done = lax.fori_loop(0, B, body, (jnp.zeros((8, L), F32),) * B, unroll=8)
    for s in range(B):
        pay_ref[s : s + 1, :] = v0_ref[s : s + 1, :] * jnp.sum(done[s], axis=0, keepdims=True)


def first_row_kernel(e_ref, got_ref, m_ref, lt_ref, pay_ref, n_ref, v0_ref):
    n = merge(got_ref)
    n_ref[...] = n
    v0_ref[...] = jnp.exp2(m_ref[...] - n + (LOG2E * lt_ref[...] + SHIFT))
    row_sums(e_ref, v0_ref, pay_ref)


def col_kernel(e_ref, got_ref, ls_ref, v0_ref, pay_ref, wide):
    spread(jnp.exp2(LOG2E * ls_ref[...]) / add_up(got_ref), wide)
    col_sums(e_ref, v0_ref, pay_ref, wide)


def row_kernel(e_ref, got_ref, lt_ref, v0_ref, pay_ref, v):
    v[...] = v0_ref[...] * (jnp.exp2(LOG2E * lt_ref[...]) / add_up(got_ref))
    row_sums(e_ref, v, pay_ref)


def last_kernel(place_ref, e_ref, got_ref, ls_ref, v0_ref, alpha_ref, sq_ref, pay_ref, f_ref, wide, total):
    total[...] = add_up(got_ref)
    own = pl.ds(pl.multiple_of(place_ref[0] * H, H), H)
    f_ref[...] = sq_ref[...] - (eps / LOG2E) * (jnp.log2(total[own, :]) - 2.0 * SHIFT - alpha_ref[own, :])
    spread(jnp.exp2(LOG2E * ls_ref[...]) / total[...], wide)
    col_sums(e_ref, v0_ref, pay_ref, wide)


def call(kernel, outs, *args, scratch=(), limit=8, aliases=None):
    return pl.pallas_call(
        kernel,
        out_shape=[pltpu.VMEM(x, F32) if isinstance(x, tuple) else x for x in outs],
        in_specs=[SM if x.dtype == jnp.int32 else VM for x in args],
        out_specs=[VM] * len(outs),
        scratch_shapes=scratch,
        input_output_aliases=aliases or {},
        compiler_params=pltpu.CompilerParams(vmem_limit_bytes=limit * 2**20),
        name=kernel.__name__,
    )(*args)


def share(x, axes):
    return lax.all_to_all(jnp.broadcast_to(x[None], (B,) + x.shape), axes, 0, 0, tiled=True)


def over_rows(x):
    return share(x, ("c", "z"))


def over_cols(x):
    return share(x, ("x", "y"))


def swap(x):
    return lax.ppermute(x, "c", [(0, 1), (1, 0)])


def climb(x, step):
    return lax.ppermute(x, "z", [(z, (z + step) % H) for z in range(H)])


def local(sources, targets, log_src_mass, log_tgt_mass):
    c = lax.axis_index("c")
    place = jnp.stack([c, lax.axis_index("z")])
    ls = log_src_mass.reshape(H, L)
    lt = lax.dynamic_index_in_dim(log_tgt_mass.reshape(B, 2, L), c, 1, keepdims=False)
    tgt = over_cols(targets).reshape(N, L)
    blocks = {0: sources, H: sources}
    for step in range(1, H // 2):
        blocks[step] = climb(blocks[step - 1], 1)
        blocks[H - step] = climb(blocks[H - step + 1], H - 1)
    blocks[H // 2] = climb(blocks[H // 2 - 1], 1)
    near = jnp.concatenate([blocks[step] for step in NEAR])
    far = jnp.concatenate([blocks[step] for step in FAR])
    wide = pltpu.VMEM((N, L), F32)
    bits = [pltpu.VMEM((N, 6 * L), BF16), pltpu.VMEM((6 * L, N), BF16), pltpu.VMEM(VEC, F32)]
    z, pay, sq, ls = call(
        start_kernel, [(N, N), VEC, (H, L), VEC], place, near, swap(near), far, swap(far), tgt, jnp.concatenate([lt, ls]), swap(ls),
        scratch=bits, limit=24,
    )
    e, pay, m, alpha = call(cols_kernel, [(N, N), VEC, VEC, VEC], z, over_rows(pay), ls, scratch=[wide], aliases={0: 0})
    pay, n, v0 = call(first_row_kernel, [VEC, VEC, VEC], e, over_cols(pay), m, lt)
    (pay,) = call(col_kernel, [VEC], e, over_rows(pay), ls, v0, scratch=[wide])
    (pay,) = call(row_kernel, [VEC], e, over_cols(pay), lt, v0, scratch=[pltpu.VMEM(VEC, F32)])
    pay, f = call(
        last_kernel, [VEC, jax.ShapeDtypeStruct((H, L), F32)], place, e, over_rows(pay), ls, v0, alpha, sq, scratch=[wide, pltpu.VMEM(VEC, F32)]
    )
    total = jnp.sum(over_cols(pay), axis=0)
    g = -eps * ((jnp.log2(total) + n) / LOG2E - 2.0 * lt)
    g = lax.all_gather(g, "c").transpose(1, 0, 2).reshape(2 * N)
    return f.reshape(N // 2), g


def solution(mesh):
    grid = Mesh(mesh.devices.reshape(4, 4, 2, 8), ("x", "y", "c", "z"))
    src, tgt = ("x", "y", "c"), "z"
    in_specs = (P((*src, tgt), None), P((tgt, *src), None), P(src), P(tgt))
    return jax.shard_map(local, mesh=grid, in_specs=in_specs, out_specs=(P(src), P(tgt)), check_vma=False)
```

profile of v0, /device:TPU:1, one launch (start us, length us, event | category | flops | bytes accessed | tf_op | source)
XLA Modules:
  0.0 136.3 jit_solution(9039982355934580017)
XLA Ops:
  0.6 0.0 copy-start
  0.6 2.5 %collective-permute-start = (f32[128,128]{1,0:T(8,128)}, f32[128,128]{1,0:T(8,128)S(1)}, u32[]{:S(2)}, u32[]{:S(2)}) collective-permute-start(f32[128,128]{1,0:T(8,128)} %param.4), channel_id=1, source_target_pairs={{0,1},{1,2},{2,3},{3,4},{4,5},{5,6},{6,7},{7,0},{8,9},{9,10},{10,1... | collective-permute-start | bytes 196616 | tf_op jit(solution)/shard_map/ppermute | solution.py:228
  3.2 4.0 %collective-permute-start.1 = (f32[128,128]{1,0:T(8,128)}, f32[128,128]{1,0:T(8,128)S(1)}, u32[]{:S(2)}, u32[]{:S(2)}) collective-permute-start(f32[128,128]{1,0:T(8,128)} %param.4), channel_id=1, source_target_pairs={{0,7},{1,0},{2,1},{3,2},{4,3},{5,4},{6,5},{7,6},{8,15},{9,8},{10,9... | collective-permute-start | bytes 196616 | tf_op jit(solution)/shard_map/ppermute | solution.py:228
  7.2 1.0 collective-permute-start.9
  8.2 1.9 %broadcast_in_dim.14 = f32[16,128,128]{2,1,0:T(8,128)} broadcast(f32[128,128]{1,0:T(8,128)} %param.5), dimensions={1,2} | broadcast | bytes 1114112 | tf_op jit(solution)/shard_map/broadcast_in_dim | solution.py:212
  10.1 6.8 %all-to-all-start = ((f32[16,128,128]{2,1,0:T(8,128)}), f32[16,128,128]{2,1,0:T(8,128)S(1)}, u32[]{:S(2)}, u32[]{:S(2)}) async-start(f32[16,128,128]{2,1,0:T(8,128)} %broadcast_in_dim.14), calls=%async_computation | async-start | bytes 2097152 | tf_op jit(solution)/shard_map/all_to_all | solution.py:212
  16.9 0.8 constant_dynamic-update-slice_fusion.4
  17.7 0.0 copy-done
  17.7 0.0 collective-permute-done
  17.7 0.1 collective-permute-start.2
  17.8 0.0 collective-permute-done.1
  17.8 2.7 %collective-permute-start.3 = (f32[128,128]{1,0:T(8,128)S(1)}, f32[128,128]{1,0:T(8,128)S(1)}, u32[]{:S(2)}, u32[]{:S(2)}) collective-permute-start(f32[128,128]{1,0:T(8,128)S(1)} %collective-permute-done.1), channel_id=1, source_target_pairs={{0,7},{1,0},{2,1},{3,2},{4,3},{5,4},{6,5},{7,6},{8,15},{9,8},{10,9... | collective-permute-start | bytes 196616 | tf_op jit(solution)/shard_map/ppermute | solution.py:228
  20.5 1.9 %collective-permute-done.2 = f32[128,128]{1,0:T(8,128)S(1)} collective-permute-done((f32[128,128]{1,0:T(8,128)S(1)}, f32[128,128]{1,0:T(8,128)S(1)}, u32[]{:S(2)}, u32[]{:S(2)}) %collective-permute-start.2) | collective-permute-done | bytes 65568 | tf_op jit(solution)/shard_map/ppermute | solution.py:228
  22.4 0.0 collective-permute-start.5
  22.5 0.0 collective-permute-done.3
  22.5 1.2 collective-permute-start.4
  23.7 3.0 %collective-permute-start.6 = (f32[128,128]{1,0:T(8,128)S(1)}, f32[128,128]{1,0:T(8,128)S(1)}, u32[]{:S(2)}, u32[]{:S(2)}) collective-permute-start(f32[128,128]{1,0:T(8,128)S(1)} %collective-permute-done.3), channel_id=1, source_target_pairs={{0,7},{1,0},{2,1},{3,2},{4,3},{5,4},{6,5},{7,6},{8,15},{9,8},{10,9... | collective-permute-start | bytes 196616 | tf_op jit(solution)/shard_map/ppermute | solution.py:228
  26.7 0.4 collective-permute-done.5
  27.1 0.0 collective-permute-start.7
  27.1 0.9 collective-permute-done.6
  28.0 3.7 %collective-permute-done.7 = f32[128,128]{1,0:T(8,128)S(1)} collective-permute-done((f32[128,128]{1,0:T(8,128)S(1)}, f32[128,128]{1,0:T(8,128)S(1)}, u32[]{:S(2)}, u32[]{:S(2)}) %collective-permute-start.7) | collective-permute-done | bytes 65568 | tf_op jit(solution)/shard_map/ppermute | solution.py:228
  31.7 2.8 %collective-permute-start.8 = (f32[384,128]{1,0:T(8,128)S(1)}, f32[384,128]{1,0:T(8,128)S(1)}, u32[]{:S(2)}, u32[]{:S(2)}) collective-permute-start(f32[384,128]{1,0:T(8,128)S(1)} %constant_dynamic-update-slice_fusion.5.far_ref), channel_id=1, source_target_pairs={{0,8},{8,0},{1,9},{9,1},{2,10},{10,2},{3,11},{11,3},{4,12},{12,4},... | collective-permute-start | bytes 589832 | tf_op jit(solution)/shard_map/ppermute | solution.py:224
  34.5 0.7 pad_maximum_fusion.mass_ref
  35.2 0.1 pad_add_fusion.place_ref
  35.3 0.0 collective-permute-done.9.ls_other_ref
  35.3 0.3 collective-permute-done.8.far_other_ref
  35.6 0.0 collective-permute-done.4.near_other_ref
  35.6 0.0 all-to-all-done
  35.6 10.5 %start_kernel.1 = (f32[2048,2048]{1,0:T(8,128)S(1)}, f32[16,128]{1,0:T(8,128)S(1)}, f32[8,128]{1,0:T(8,128)S(1)}, f32[16,128]{1,0:T(8,128)S(1)}) custom-call(s32[2]{0:T(128)S(1)} %pad_add_fusion.place_ref, f32[640,128]{1,0:T(8,128)S(1)} %constant_dynamic-update-slice_fusion.near_ref, f32[640,128]{1,0:T(8,128)S(1)} %collective-permute-done.4.near_other_ref, ...), custom_call_target="tpu_custom_call" | custom-call | tf_op jit(solution)/shard_map/start_kernel/pallas_call | solution.py:199
  46.2 13.2 %all_to_all.35.got_ref = f32[16,16,128]{2,1,0:T(8,128)S(1)} all-to-all(f32[16,16,128]{2,1,0:T(8,128)S(1)} %broadcast_in_dim.15), channel_id=1, replica_groups=mesh['x'=4,'y'=4,'c'=2,'z'=8] {'c','z'}, dimensions={0} | all-to-all | bytes 262144 | tf_op jit(solution)/shard_map/all_to_all | solution.py:212
  59.4 6.0 %cols_kernel.1 = (f32[2048,2048]{1,0:T(8,128)S(1)}, f32[16,128]{1,0:T(8,128)S(1)}, f32[16,128]{1,0:T(8,128)S(1)}, f32[16,128]{1,0:T(8,128)S(1)}) custom-call(f32[2048,2048]{1,0:T(8,128)S(1)} %get-tuple-element.15.z_ref, f32[16,16,128]{2,1,0:T(8,128)S(1)} %all_to_all.35.got_ref, f32[16,128]{1,0:T(8,128)S(1)} %get-tuple-element.17.ls_ref), custom_call_target="tpu_custom_call", output_to_operand_aliasing={{0}: (0, {})} | custom-call | tf_op jit(solution)/shard_map/cols_kernel/pallas_call | solution.py:199
  65.4 13.4 %all_to_all.36.got_ref = f32[16,16,128]{2,1,0:T(8,128)S(1)} all-to-all(f32[16,16,128]{2,1,0:T(8,128)S(1)} %broadcast_in_dim.16), channel_id=1, replica_groups=mesh['x'=4,'y'=4,'c'=2,'z'=8] {'x','y'}, dimensions={0} | all-to-all | bytes 262144 | tf_op jit(solution)/shard_map/all_to_all | solution.py:212
  78.9 1.4 %first_row_kernel.1 = (f32[16,128]{1,0:T(8,128)S(1)}, f32[16,128]{1,0:T(8,128)S(1)}, f32[16,128]{1,0:T(8,128)S(1)}) custom-call(f32[2048,2048]{1,0:T(8,128)S(1)} %get-tuple-element.18.e_ref, f32[16,16,128]{2,1,0:T(8,128)S(1)} %all_to_all.36.got_ref, f32[16,128]{1,0:T(8,128)S(1)} %get-tuple-element.20.m_ref, f32[16,128]{1,0:T(8,128)S(1)} %bitcast.14), custom_call_target="tpu_custom_call" | custom-call | tf_op jit(solution)/shard_map/first_row_kernel/pallas_call | solution.py:199
  80.3 13.0 %all_to_all.37.got_ref = f32[16,16,128]{2,1,0:T(8,128)S(1)} all-to-all(f32[16,16,128]{2,1,0:T(8,128)S(1)} %broadcast_in_dim.17), channel_id=1, replica_groups=mesh['x'=4,'y'=4,'c'=2,'z'=8] {'c','z'}, dimensions={0} | all-to-all | bytes 262144 | tf_op jit(solution)/shard_map/all_to_all | solution.py:212
  93.3 1.8 %col_kernel.1 = f32[16,128]{1,0:T(8,128)S(1)} custom-call(f32[2048,2048]{1,0:T(8,128)S(1)} %get-tuple-element.18.e_ref, f32[16,16,128]{2,1,0:T(8,128)S(1)} %all_to_all.37.got_ref, f32[16,128]{1,0:T(8,128)S(1)} %get-tuple-element.17.ls_ref, f32[16,128]{1,0:T(8,128)S(1)} %get-tuple-element.22.v0_ref), custom_call_target="tpu_custom_call" | custom-call | tf_op jit(solution)/shard_map/col_kernel/pallas_call | solution.py:199
  95.1 9.8 %all_to_all.38.got_ref = f32[16,16,128]{2,1,0:T(8,128)S(1)} all-to-all(f32[16,16,128]{2,1,0:T(8,128)S(1)} %broadcast_in_dim.18), channel_id=1, replica_groups=mesh['x'=4,'y'=4,'c'=2,'z'=8] {'x','y'}, dimensions={0} | all-to-all | bytes 262144 | tf_op jit(solution)/shard_map/all_to_all | solution.py:212
  104.9 1.4 row_kernel.1
  106.3 13.0 %all_to_all.39.got_ref = f32[16,16,128]{2,1,0:T(8,128)S(1)} all-to-all(f32[16,16,128]{2,1,0:T(8,128)S(1)} %broadcast_in_dim.19), channel_id=1, replica_groups=mesh['x'=4,'y'=4,'c'=2,'z'=8] {'c','z'}, dimensions={0} | all-to-all | bytes 262144 | tf_op jit(solution)/shard_map/all_to_all | solution.py:212
  119.3 2.3 %last_kernel.1 = (f32[16,128]{1,0:T(8,128)S(1)}, f32[8,128]{1,0:T(8,128)}) custom-call(s32[2]{0:T(128)S(1)} %pad_add_fusion.place_ref, f32[2048,2048]{1,0:T(8,128)S(1)} %get-tuple-element.18.e_ref, f32[16,16,128]{2,1,0:T(8,128)S(1)} %all_to_all.39.got_ref, f32[16,128]{1,0:T(8,128)S(1)} %get-tuple-element.17.ls_ref, f32[16,128]{1,0:T(8,128)S(1)} %get-tuple-element.22.v0_ref, ...), custom_call_target="tpu_custom_call" | custom-call | tf_op jit(solution)/shard_map/last_kernel/pallas_call | solution.py:199
  121.6 9.8 %all_to_all.40 = f32[16,16,128]{2,1,0:T(8,128)S(1)} all-to-all(f32[16,16,128]{2,1,0:T(8,128)S(1)} %broadcast_in_dim.20), channel_id=1, replica_groups=mesh['x'=4,'y'=4,'c'=2,'z'=8] {'x','y'}, dimensions={0} | all-to-all | bytes 262144 | tf_op jit(solution)/shard_map/all_to_all | solution.py:212
  131.5 4.2 %all-gather = f32[32,128]{1,0:T(8,128)S(1)} all-gather(f32[16,128]{1,0:T(8,128)S(1)} %subtract_multiply_fusion), channel_id=2, replica_groups=mesh['x'=4,'y'=4,'c'=2,'z'=8] {'c'}, dimensions={0}, use_global_device_ids=true | all-gather | bytes 24576 | tf_op jit(solution)/shard_map/all_gather | solution.py:259
  135.7 0.6 copy.8
  (16 shorter events, 0.1 us)
Async XLA Ops:
  0.6 17.1 %copy-start = (f32[4096]{0:T(1024)S(1)}, f32[4096]{0:T(1024)}, u32[]{:S(2)}) copy-start(f32[4096]{0:T(1024)} %param.7) | copy-start | bytes 49156
  0.6 17.1 %collective-permute-start = (f32[128,128]{1,0:T(8,128)}, f32[128,128]{1,0:T(8,128)S(1)}, u32[]{:S(2)}, u32[]{:S(2)}) collective-permute-start(f32[128,128]{1,0:T(8,128)} %param.4), channel_id=1, source_target_pairs={{0,1},{1,2},{2,3},{3,4},{4,5},{5,6},{6,7},{7,0},{8,9},{9,10},{10,1... | collective-permute-start | bytes 196616 | tf_op jit(solution)/shard_map/ppermute | solution.py:228
  3.2 14.6 %collective-permute-start.1 = (f32[128,128]{1,0:T(8,128)}, f32[128,128]{1,0:T(8,128)S(1)}, u32[]{:S(2)}, u32[]{:S(2)}) collective-permute-start(f32[128,128]{1,0:T(8,128)} %param.4), channel_id=1, source_target_pairs={{0,7},{1,0},{2,1},{3,2},{4,3},{5,4},{6,5},{7,6},{8,15},{9,8},{10,9... | collective-permute-start | bytes 196616 | tf_op jit(solution)/shard_map/ppermute | solution.py:228
  7.2 28.1 %collective-permute-start.9 = (f32[8,128]{1,0:T(8,128)}, f32[8,128]{1,0:T(8,128)S(1)}, u32[]{:S(2)}, u32[]{:S(2)}) collective-permute-start(f32[8,128]{1,0:T(8,128)} %bitcast.19), channel_id=1, source_target_pairs={{0,8},{8,0},{1,9},{9,1},{2,10},{10,2},{3,11},{11,3},{4,12},{12,4},... | collective-permute-start | bytes 12296 | tf_op jit(solution)/shard_map/ppermute | solution.py:224
  10.1 25.5 %all-to-all-start = ((f32[16,128,128]{2,1,0:T(8,128)}), f32[16,128,128]{2,1,0:T(8,128)S(1)}, u32[]{:S(2)}, u32[]{:S(2)}) async-start(f32[16,128,128]{2,1,0:T(8,128)} %broadcast_in_dim.14), calls=%async_computation | async-start | bytes 2097152 | tf_op jit(solution)/shard_map/all_to_all | solution.py:212
  17.7 4.7 %collective-permute-start.2 = (f32[128,128]{1,0:T(8,128)S(1)}, f32[128,128]{1,0:T(8,128)S(1)}, u32[]{:S(2)}, u32[]{:S(2)}) collective-permute-start(f32[128,128]{1,0:T(8,128)S(1)} %collective-permute-done), channel_id=1, source_target_pairs={{0,1},{1,2},{2,3},{3,4},{4,5},{5,6},{6,7},{7,0},{8,9},{9,10},{10,1... | collective-permute-start | bytes 196616 | tf_op jit(solution)/shard_map/ppermute | solution.py:228
  17.8 4.6 %collective-permute-start.3 = (f32[128,128]{1,0:T(8,128)S(1)}, f32[128,128]{1,0:T(8,128)S(1)}, u32[]{:S(2)}, u32[]{:S(2)}) collective-permute-start(f32[128,128]{1,0:T(8,128)S(1)} %collective-permute-done.1), channel_id=1, source_target_pairs={{0,7},{1,0},{2,1},{3,2},{4,3},{5,4},{6,5},{7,6},{8,15},{9,8},{10,9... | collective-permute-start | bytes 196616 | tf_op jit(solution)/shard_map/ppermute | solution.py:228
  22.4 4.6 %collective-permute-start.5 = (f32[128,128]{1,0:T(8,128)S(1)}, f32[128,128]{1,0:T(8,128)S(1)}, u32[]{:S(2)}, u32[]{:S(2)}) collective-permute-start(f32[128,128]{1,0:T(8,128)S(1)} %collective-permute-done.2), channel_id=1, source_target_pairs={{0,1},{1,2},{2,3},{3,4},{4,5},{5,6},{6,7},{7,0},{8,9},{9,10},{10,1... | collective-permute-start | bytes 196616 | tf_op jit(solution)/shard_map/ppermute | solution.py:228
  22.5 13.1 %collective-permute-start.4 = (f32[640,128]{1,0:T(8,128)S(1)}, f32[640,128]{1,0:T(8,128)S(1)}, u32[]{:S(2)}, u32[]{:S(2)}) collective-permute-start(f32[640,128]{1,0:T(8,128)S(1)} %constant_dynamic-update-slice_fusion.near_ref), channel_id=1, source_target_pairs={{0,8},{8,0},{1,9},{9,1},{2,10},{10,2},{3,11},{11,3},{4,12},{12,4},... | collective-permute-start | bytes 983048 | tf_op jit(solution)/shard_map/ppermute | solution.py:224
  23.7 4.3 %collective-permute-start.6 = (f32[128,128]{1,0:T(8,128)S(1)}, f32[128,128]{1,0:T(8,128)S(1)}, u32[]{:S(2)}, u32[]{:S(2)}) collective-permute-start(f32[128,128]{1,0:T(8,128)S(1)} %collective-permute-done.3), channel_id=1, source_target_pairs={{0,7},{1,0},{2,1},{3,2},{4,3},{5,4},{6,5},{7,6},{8,15},{9,8},{10,9... | collective-permute-start | bytes 196616 | tf_op jit(solution)/shard_map/ppermute | solution.py:228
  27.1 4.6 %collective-permute-start.7 = (f32[128,128]{1,0:T(8,128)S(1)}, f32[128,128]{1,0:T(8,128)S(1)}, u32[]{:S(2)}, u32[]{:S(2)}) collective-permute-start(f32[128,128]{1,0:T(8,128)S(1)} %collective-permute-done.5), channel_id=1, source_target_pairs={{0,1},{1,2},{2,3},{3,4},{4,5},{5,6},{6,7},{7,0},{8,9},{9,10},{10,1... | collective-permute-start | bytes 196616 | tf_op jit(solution)/shard_map/ppermute | solution.py:228
  31.7 3.9 %collective-permute-start.8 = (f32[384,128]{1,0:T(8,128)S(1)}, f32[384,128]{1,0:T(8,128)S(1)}, u32[]{:S(2)}, u32[]{:S(2)}) collective-permute-start(f32[384,128]{1,0:T(8,128)S(1)} %constant_dynamic-update-slice_fusion.5.far_ref), channel_id=1, source_target_pairs={{0,8},{8,0},{1,9},{9,1},{2,10},{10,2},{3,11},{11,3},{4,12},{12,4},... | collective-permute-start | bytes 589832 | tf_op jit(solution)/shard_map/ppermute | solution.py:224
where the time goes:
time: 137 us; the launch traced here: 136 us
  blocking collectives  76.5 us (56%)
  starting transfers between devices  24.1 us (18%)
  Pallas kernels  23.4 us (17%)
  waiting for transfers between devices  7.25 us (5%)
  local copies, waits for them, and re-layouts  3.51 us (3%)
    all_to_all x6, blocking collectives, share(): lax.all_to_all(jnp.broadcast_to(x[None], (B,) + x.shape), axes, 0, 0, til...  72.3 us
    pallas_call x6, Pallas kernels, call(): pl.pallas_call(kernel, out_shape=[pltpu.VMEM(x, F32) if isinstance(x, tup...  23.4 us
    ppermute x7, starting transfers between devices, climb(): return lax.ppermute(x, 'z', [(z, (z + step) % H) for z in range(H)])  12.3 us
    ppermute x7, waiting for transfers between devices, climb(): return lax.ppermute(x, 'z', [(z, (z + step) % H) for z in range(H)])  6.93 us
    all_to_all x1, starting transfers between devices, share(): lax.all_to_all(jnp.broadcast_to(x[None], (B,) + x.shape), axes, 0, 0, til...  6.75 us
    ppermute x3, starting transfers between devices, swap(): return lax.ppermute(x, 'c', [(0, 1), (1, 0)])  5.03 us
    all_gather x1, blocking collectives, local(): g = lax.all_gather(g, 'c').transpose(1, 0, 2).reshape(2 * N)  4.2 us
  transfers between devices with their start and end apart: 11, of which 5 were waited for; matrix products, arithmetic and copies ran while one was open for 3% of the time, Pallas kernels for 0%

commit v1 on v0

--- a/solution.py
+++ b/solution.py
@@ -238,7 +238,7 @@
     for step in range(1, H // 2):
         blocks[step] = climb(blocks[step - 1], 1)
         blocks[H - step] = climb(blocks[H - step + 1], H - 1)
-    blocks[H // 2] = climb(blocks[H // 2 - 1], 1)
+    blocks[H // 2] = climb(blocks[H // 2 - 2], 2)
     near = jnp.concatenate([blocks[step] for step in NEAR])
     far = jnp.concatenate([blocks[step] for step in FAR])
     wide = pltpu.VMEM((N, L), F32)

time: 137 us -> 134 us (0.978)
  starting transfers between devices: 24.1 us -> 22.3 us
    ppermute x3, starting transfers between devices: 5.03 us -> 3.31 us  [swap(): return lax.ppermute(x, 'c', [(0, 1), (1, 0)])]
where the time goes in v1:
time: 134 us
  blocking collectives  75.5 us (56%)
  Pallas kernels  23.4 us (17%)
  starting transfers between devices  22.3 us (17%)
  waiting for transfers between devices  7.22 us (5%)
  local copies, waits for them, and re-layouts  3.51 us (3%)
    all_to_all x6, blocking collectives, share(): lax.all_to_all(jnp.broadcast_to(x[None], (B,) + x.shape), axes, 0, 0, til...  71.3 us
    pallas_call x6, Pallas kernels, call(): pl.pallas_call(kernel, out_shape=[pltpu.VMEM(x, F32) if isinstance(x, tup...  23.4 us
    ppermute x7, starting transfers between devices, climb(): return lax.ppermute(x, 'z', [(z, (z + step) % H) for z in range(H)])  12.3 us
    all_to_all x1, starting transfers between devices, share(): lax.all_to_all(jnp.broadcast_to(x[None], (B,) + x.shape), axes, 0, 0, til...  6.75 us
    ppermute x7, waiting for transfers between devices, climb(): return lax.ppermute(x, 'z', [(z, (z + step) % H) for z in range(H)])  6.21 us
    all_gather x1, blocking collectives, local(): g = lax.all_gather(g, 'c').transpose(1, 0, 2).reshape(2 * N)  4.2 us
    ppermute x3, starting transfers between devices, swap(): return lax.ppermute(x, 'c', [(0, 1), (1, 0)])  3.31 us
  transfers between devices with their start and end apart: 11, of which 5 were waited for; matrix products, arithmetic and copies ran while one was open for 3% of the time, Pallas kernels for 0%

profile of v1, /device:TPU:1, one launch (start us, length us, event | category | flops | bytes accessed | tf_op | source)
XLA Modules:
  0.0 133.6 jit_solution(10741002959299474370)
XLA Ops:
  0.6 0.0 copy-start
  0.6 2.5 %collective-permute-start = (f32[128,128]{1,0:T(8,128)}, f32[128,128]{1,0:T(8,128)S(1)}, u32[]{:S(2)}, u32[]{:S(2)}) collective-permute-start(f32[128,128]{1,0:T(8,128)} %param.4), channel_id=1, source_target_pairs={{0,1},{1,2},{2,3},{3,4},{4,5},{5,6},{6,7},{7,0},{8,9},{9,10},{10,1... | collective-permute-start | bytes 196616 | tf_op jit(solution)/shard_map/ppermute | solution.py:228
  3.2 4.0 %collective-permute-start.1 = (f32[128,128]{1,0:T(8,128)}, f32[128,128]{1,0:T(8,128)S(1)}, u32[]{:S(2)}, u32[]{:S(2)}) collective-permute-start(f32[128,128]{1,0:T(8,128)} %param.4), channel_id=1, source_target_pairs={{0,7},{1,0},{2,1},{3,2},{4,3},{5,4},{6,5},{7,6},{8,15},{9,8},{10,9... | collective-permute-start | bytes 196616 | tf_op jit(solution)/shard_map/ppermute | solution.py:228
  7.2 1.0 collective-permute-start.9
  8.2 1.9 %broadcast_in_dim.14 = f32[16,128,128]{2,1,0:T(8,128)} broadcast(f32[128,128]{1,0:T(8,128)} %param.5), dimensions={1,2} | broadcast | bytes 1114112 | tf_op jit(solution)/shard_map/broadcast_in_dim | solution.py:212
  10.1 6.8 %all-to-all-start = ((f32[16,128,128]{2,1,0:T(8,128)}), f32[16,128,128]{2,1,0:T(8,128)S(1)}, u32[]{:S(2)}, u32[]{:S(2)}) async-start(f32[16,128,128]{2,1,0:T(8,128)} %broadcast_in_dim.14), calls=%async_computation | async-start | bytes 2097152 | tf_op jit(solution)/shard_map/all_to_all | solution.py:212
  16.9 0.8 constant_dynamic-update-slice_fusion.4
  17.7 0.0 copy-done
  17.7 0.0 collective-permute-done
  17.7 0.1 collective-permute-start.2
  17.8 0.0 collective-permute-done.1
  17.8 2.7 %collective-permute-start.3 = (f32[128,128]{1,0:T(8,128)S(1)}, f32[128,128]{1,0:T(8,128)S(1)}, u32[]{:S(2)}, u32[]{:S(2)}) collective-permute-start(f32[128,128]{1,0:T(8,128)S(1)} %collective-permute-done.1), channel_id=1, source_target_pairs={{0,7},{1,0},{2,1},{3,2},{4,3},{5,4},{6,5},{7,6},{8,15},{9,8},{10,9... | collective-permute-start | bytes 196616 | tf_op jit(solution)/shard_map/ppermute | solution.py:228
  20.5 1.9 %collective-permute-done.2 = f32[128,128]{1,0:T(8,128)S(1)} collective-permute-done((f32[128,128]{1,0:T(8,128)S(1)}, f32[128,128]{1,0:T(8,128)S(1)}, u32[]{:S(2)}, u32[]{:S(2)}) %collective-permute-start.2) | collective-permute-done | bytes 65568 | tf_op jit(solution)/shard_map/ppermute | solution.py:228
  22.4 0.0 collective-permute-start.5
  22.5 0.0 collective-permute-done.3
  22.5 1.2 collective-permute-start.4
  23.7 2.0 %collective-permute-start.7 = (f32[128,128]{1,0:T(8,128)S(1)}, f32[128,128]{1,0:T(8,128)S(1)}, u32[]{:S(2)}, u32[]{:S(2)}) collective-permute-start(f32[128,128]{1,0:T(8,128)S(1)} %collective-permute-done.2), channel_id=1, source_target_pairs={{0,2},{1,3},{2,4},{3,5},{4,6},{5,7},{6,0},{7,1},{8,10},{9,11},{10,... | collective-permute-start | bytes 196616 | tf_op jit(solution)/shard_map/ppermute | solution.py:228
  25.7 1.0 collective-permute-start.6
  26.7 0.4 collective-permute-done.5
  27.1 3.9 %collective-permute-done.6 = f32[128,128]{1,0:T(8,128)S(1)} collective-permute-done((f32[128,128]{1,0:T(8,128)S(1)}, f32[128,128]{1,0:T(8,128)S(1)}, u32[]{:S(2)}, u32[]{:S(2)}) %collective-permute-start.6) | collective-permute-done | bytes 65568 | tf_op jit(solution)/shard_map/ppermute | solution.py:228
  30.9 0.0 collective-permute-done.7
  31.0 1.1 collective-permute-start.8
  32.1 0.7 pad_maximum_fusion.mass_ref
  32.8 0.1 pad_add_fusion.place_ref
  32.9 0.0 collective-permute-done.9.ls_other_ref
  32.9 0.3 collective-permute-done.8.far_other_ref
  33.2 0.0 collective-permute-done.4.near_other_ref
  33.2 0.7 all-to-all-done
  33.9 10.5 %start_kernel.1 = (f32[2048,2048]{1,0:T(8,128)S(1)}, f32[16,128]{1,0:T(8,128)S(1)}, f32[8,128]{1,0:T(8,128)S(1)}, f32[16,128]{1,0:T(8,128)S(1)}) custom-call(s32[2]{0:T(128)S(1)} %pad_add_fusion.place_ref, f32[640,128]{1,0:T(8,128)S(1)} %constant_dynamic-update-slice_fusion.near_ref, f32[640,128]{1,0:T(8,128)S(1)} %collective-permute-done.4.near_other_ref, ...), custom_call_target="tpu_custom_call" | custom-call | tf_op jit(solution)/shard_map/start_kernel/pallas_call | solution.py:199
  44.4 14.6 %all_to_all.35.got_ref = f32[16,16,128]{2,1,0:T(8,128)S(1)} all-to-all(f32[16,16,128]{2,1,0:T(8,128)S(1)} %broadcast_in_dim.15), channel_id=1, replica_groups=mesh['x'=4,'y'=4,'c'=2,'z'=8] {'c','z'}, dimensions={0} | all-to-all | bytes 262144 | tf_op jit(solution)/shard_map/all_to_all | solution.py:212
  59.0 6.0 %cols_kernel.1 = (f32[2048,2048]{1,0:T(8,128)S(1)}, f32[16,128]{1,0:T(8,128)S(1)}, f32[16,128]{1,0:T(8,128)S(1)}, f32[16,128]{1,0:T(8,128)S(1)}) custom-call(f32[2048,2048]{1,0:T(8,128)S(1)} %get-tuple-element.15.z_ref, f32[16,16,128]{2,1,0:T(8,128)S(1)} %all_to_all.35.got_ref, f32[16,128]{1,0:T(8,128)S(1)} %get-tuple-element.17.ls_ref), custom_call_target="tpu_custom_call", output_to_operand_aliasing={{0}: (0, {})} | custom-call | tf_op jit(solution)/shard_map/cols_kernel/pallas_call | solution.py:199
  65.1 11.1 %all_to_all.36.got_ref = f32[16,16,128]{2,1,0:T(8,128)S(1)} all-to-all(f32[16,16,128]{2,1,0:T(8,128)S(1)} %broadcast_in_dim.16), channel_id=1, replica_groups=mesh['x'=4,'y'=4,'c'=2,'z'=8] {'x','y'}, dimensions={0} | all-to-all | bytes 262144 | tf_op jit(solution)/shard_map/all_to_all | solution.py:212
  76.1 1.4 %first_row_kernel.1 = (f32[16,128]{1,0:T(8,128)S(1)}, f32[16,128]{1,0:T(8,128)S(1)}, f32[16,128]{1,0:T(8,128)S(1)}) custom-call(f32[2048,2048]{1,0:T(8,128)S(1)} %get-tuple-element.18.e_ref, f32[16,16,128]{2,1,0:T(8,128)S(1)} %all_to_all.36.got_ref, f32[16,128]{1,0:T(8,128)S(1)} %get-tuple-element.20.m_ref, f32[16,128]{1,0:T(8,128)S(1)} %bitcast.14), custom_call_target="tpu_custom_call" | custom-call | tf_op jit(solution)/shard_map/first_row_kernel/pallas_call | solution.py:199
  77.5 13.0 %all_to_all.37.got_ref = f32[16,16,128]{2,1,0:T(8,128)S(1)} all-to-all(f32[16,16,128]{2,1,0:T(8,128)S(1)} %broadcast_in_dim.17), channel_id=1, replica_groups=mesh['x'=4,'y'=4,'c'=2,'z'=8] {'c','z'}, dimensions={0} | all-to-all | bytes 262144 | tf_op jit(solution)/shard_map/all_to_all | solution.py:212
  90.5 1.8 %col_kernel.1 = f32[16,128]{1,0:T(8,128)S(1)} custom-call(f32[2048,2048]{1,0:T(8,128)S(1)} %get-tuple-element.18.e_ref, f32[16,16,128]{2,1,0:T(8,128)S(1)} %all_to_all.37.got_ref, f32[16,128]{1,0:T(8,128)S(1)} %get-tuple-element.17.ls_ref, f32[16,128]{1,0:T(8,128)S(1)} %get-tuple-element.22.v0_ref), custom_call_target="tpu_custom_call" | custom-call | tf_op jit(solution)/shard_map/col_kernel/pallas_call | solution.py:199
  92.3 9.8 %all_to_all.38.got_ref = f32[16,16,128]{2,1,0:T(8,128)S(1)} all-to-all(f32[16,16,128]{2,1,0:T(8,128)S(1)} %broadcast_in_dim.18), channel_id=1, replica_groups=mesh['x'=4,'y'=4,'c'=2,'z'=8] {'x','y'}, dimensions={0} | all-to-all | bytes 262144 | tf_op jit(solution)/shard_map/all_to_all | solution.py:212
  102.2 1.4 %row_kernel.1 = f32[16,128]{1,0:T(8,128)S(1)} custom-call(f32[2048,2048]{1,0:T(8,128)S(1)} %get-tuple-element.18.e_ref, f32[16,16,128]{2,1,0:T(8,128)S(1)} %all_to_all.38.got_ref, f32[16,128]{1,0:T(8,128)S(1)} %bitcast.15, f32[16,128]{1,0:T(8,128)S(1)} %get-tuple-element.22.v0_ref), custom_call_target="tpu_custom_call" | custom-call | tf_op jit(solution)/shard_map/row_kernel/pallas_call | solution.py:199
  103.5 13.0 %all_to_all.39.got_ref = f32[16,16,128]{2,1,0:T(8,128)S(1)} all-to-all(f32[16,16,128]{2,1,0:T(8,128)S(1)} %broadcast_in_dim.19), channel_id=1, replica_groups=mesh['x'=4,'y'=4,'c'=2,'z'=8] {'c','z'}, dimensions={0} | all-to-all | bytes 262144 | tf_op jit(solution)/shard_map/all_to_all | solution.py:212
  116.6 2.3 %last_kernel.1 = (f32[16,128]{1,0:T(8,128)S(1)}, f32[8,128]{1,0:T(8,128)}) custom-call(s32[2]{0:T(128)S(1)} %pad_add_fusion.place_ref, f32[2048,2048]{1,0:T(8,128)S(1)} %get-tuple-element.18.e_ref, f32[16,16,128]{2,1,0:T(8,128)S(1)} %all_to_all.39.got_ref, f32[16,128]{1,0:T(8,128)S(1)} %get-tuple-element.17.ls_ref, f32[16,128]{1,0:T(8,128)S(1)} %get-tuple-element.22.v0_ref, ...), custom_call_target="tpu_custom_call" | custom-call | tf_op jit(solution)/shard_map/last_kernel/pallas_call | solution.py:199
  118.9 9.8 %all_to_all.40 = f32[16,16,128]{2,1,0:T(8,128)S(1)} all-to-all(f32[16,16,128]{2,1,0:T(8,128)S(1)} %broadcast_in_dim.20), channel_id=1, replica_groups=mesh['x'=4,'y'=4,'c'=2,'z'=8] {'x','y'}, dimensions={0} | all-to-all | bytes 262144 | tf_op jit(solution)/shard_map/all_to_all | solution.py:212
  128.8 4.2 %all-gather = f32[32,128]{1,0:T(8,128)S(1)} all-gather(f32[16,128]{1,0:T(8,128)S(1)} %subtract_multiply_fusion), channel_id=2, replica_groups=mesh['x'=4,'y'=4,'c'=2,'z'=8] {'c'}, dimensions={0}, use_global_device_ids=true | all-gather | bytes 24576 | tf_op jit(solution)/shard_map/all_gather | solution.py:259
  133.0 0.6 copy.8
  (16 shorter events, 0.1 us)
Async XLA Ops:
  0.6 17.1 %copy-start = (f32[4096]{0:T(1024)S(1)}, f32[4096]{0:T(1024)}, u32[]{:S(2)}) copy-start(f32[4096]{0:T(1024)} %param.7) | copy-start | bytes 49156
  0.6 17.1 %collective-permute-start = (f32[128,128]{1,0:T(8,128)}, f32[128,128]{1,0:T(8,128)S(1)}, u32[]{:S(2)}, u32[]{:S(2)}) collective-permute-start(f32[128,128]{1,0:T(8,128)} %param.4), channel_id=1, source_target_pairs={{0,1},{1,2},{2,3},{3,4},{4,5},{5,6},{6,7},{7,0},{8,9},{9,10},{10,1... | collective-permute-start | bytes 196616 | tf_op jit(solution)/shard_map/ppermute | solution.py:228
  3.2 14.6 %collective-permute-start.1 = (f32[128,128]{1,0:T(8,128)}, f32[128,128]{1,0:T(8,128)S(1)}, u32[]{:S(2)}, u32[]{:S(2)}) collective-permute-start(f32[128,128]{1,0:T(8,128)} %param.4), channel_id=1, source_target_pairs={{0,7},{1,0},{2,1},{3,2},{4,3},{5,4},{6,5},{7,6},{8,15},{9,8},{10,9... | collective-permute-start | bytes 196616 | tf_op jit(solution)/shard_map/ppermute | solution.py:228
  7.2 25.6 %collective-permute-start.9 = (f32[8,128]{1,0:T(8,128)}, f32[8,128]{1,0:T(8,128)S(1)}, u32[]{:S(2)}, u32[]{:S(2)}) collective-permute-start(f32[8,128]{1,0:T(8,128)} %bitcast.19), channel_id=1, source_target_pairs={{0,8},{8,0},{1,9},{9,1},{2,10},{10,2},{3,11},{11,3},{4,12},{12,4},... | collective-permute-start | bytes 12296 | tf_op jit(solution)/shard_map/ppermute | solution.py:224
  10.1 23.8 %all-to-all-start = ((f32[16,128,128]{2,1,0:T(8,128)}), f32[16,128,128]{2,1,0:T(8,128)S(1)}, u32[]{:S(2)}, u32[]{:S(2)}) async-start(f32[16,128,128]{2,1,0:T(8,128)} %broadcast_in_dim.14), calls=%async_computation | async-start | bytes 2097152 | tf_op jit(solution)/shard_map/all_to_all | solution.py:212
  17.7 4.7 %collective-permute-start.2 = (f32[128,128]{1,0:T(8,128)S(1)}, f32[128,128]{1,0:T(8,128)S(1)}, u32[]{:S(2)}, u32[]{:S(2)}) collective-permute-start(f32[128,128]{1,0:T(8,128)S(1)} %collective-permute-done), channel_id=1, source_target_pairs={{0,1},{1,2},{2,3},{3,4},{4,5},{5,6},{6,7},{7,0},{8,9},{9,10},{10,1... | collective-permute-start | bytes 196616 | tf_op jit(solution)/shard_map/ppermute | solution.py:228
  17.8 4.6 %collective-permute-start.3 = (f32[128,128]{1,0:T(8,128)S(1)}, f32[128,128]{1,0:T(8,128)S(1)}, u32[]{:S(2)}, u32[]{:S(2)}) collective-permute-start(f32[128,128]{1,0:T(8,128)S(1)} %collective-permute-done.1), channel_id=1, source_target_pairs={{0,7},{1,0},{2,1},{3,2},{4,3},{5,4},{6,5},{7,6},{8,15},{9,8},{10,9... | collective-permute-start | bytes 196616 | tf_op jit(solution)/shard_map/ppermute | solution.py:228
  22.4 4.6 %collective-permute-start.5 = (f32[128,128]{1,0:T(8,128)S(1)}, f32[128,128]{1,0:T(8,128)S(1)}, u32[]{:S(2)}, u32[]{:S(2)}) collective-permute-start(f32[128,128]{1,0:T(8,128)S(1)} %collective-permute-done.2), channel_id=1, source_target_pairs={{0,1},{1,2},{2,3},{3,4},{4,5},{5,6},{6,7},{7,0},{8,9},{9,10},{10,1... | collective-permute-start | bytes 196616 | tf_op jit(solution)/shard_map/ppermute | solution.py:228
  22.5 10.7 %collective-permute-start.4 = (f32[640,128]{1,0:T(8,128)S(1)}, f32[640,128]{1,0:T(8,128)S(1)}, u32[]{:S(2)}, u32[]{:S(2)}) collective-permute-start(f32[640,128]{1,0:T(8,128)S(1)} %constant_dynamic-update-slice_fusion.near_ref), channel_id=1, source_target_pairs={{0,8},{8,0},{1,9},{9,1},{2,10},{10,2},{3,11},{11,3},{4,12},{12,4},... | collective-permute-start | bytes 983048 | tf_op jit(solution)/shard_map/ppermute | solution.py:224
  23.7 7.2 %collective-permute-start.7 = (f32[128,128]{1,0:T(8,128)S(1)}, f32[128,128]{1,0:T(8,128)S(1)}, u32[]{:S(2)}, u32[]{:S(2)}) collective-permute-start(f32[128,128]{1,0:T(8,128)S(1)} %collective-permute-done.2), channel_id=1, source_target_pairs={{0,2},{1,3},{2,4},{3,5},{4,6},{5,7},{6,0},{7,1},{8,10},{9,11},{10,... | collective-permute-start | bytes 196616 | tf_op jit(solution)/shard_map/ppermute | solution.py:228
  25.7 5.2 %collective-permute-start.6 = (f32[128,128]{1,0:T(8,128)S(1)}, f32[128,128]{1,0:T(8,128)S(1)}, u32[]{:S(2)}, u32[]{:S(2)}) collective-permute-start(f32[128,128]{1,0:T(8,128)S(1)} %collective-permute-done.3), channel_id=1, source_target_pairs={{0,7},{1,0},{2,1},{3,2},{4,3},{5,4},{6,5},{7,6},{8,15},{9,8},{10,9... | collective-permute-start | bytes 196616 | tf_op jit(solution)/shard_map/ppermute | solution.py:228
  31.0 2.2 %collective-permute-start.8 = (f32[384,128]{1,0:T(8,128)S(1)}, f32[384,128]{1,0:T(8,128)S(1)}, u32[]{:S(2)}, u32[]{:S(2)}) collective-permute-start(f32[384,128]{1,0:T(8,128)S(1)} %constant_dynamic-update-slice_fusion.5.far_ref), channel_id=1, source_target_pairs={{0,8},{8,0},{1,9},{9,1},{2,10},{10,2},{3,11},{11,3},{4,12},{12,4},... | collective-permute-start | bytes 589832 | tf_op jit(solution)/shard_map/ppermute | solution.py:224

commit v2 on v1

--- a/solution.py
+++ b/solution.py
@@ -22,8 +22,8 @@
 VM = pl.BlockSpec(memory_space=pltpu.VMEM)
 SM = pl.BlockSpec(memory_space=pltpu.SMEM)
 VEC = (B, L)
-NEAR = (0, 1, 7, 2, 6)
-FAR = (3, 5, 4)
+NEAR = (1, 7, 2, 6)
+FAR = (0, 3, 5, 4)
 PARTS = ((0, 0), (0, 1), (1, 0), (1, 1), (0, 2), (2, 0))
 
 
@@ -239,6 +239,7 @@
         blocks[step] = climb(blocks[step - 1], 1)
         blocks[H - step] = climb(blocks[H - step + 1], H - 1)
     blocks[H // 2] = climb(blocks[H // 2 - 2], 2)
+    blocks[0], blocks[2] = lax.optimization_barrier((sources, blocks[2]))
     near = jnp.concatenate([blocks[step] for step in NEAR])
     far = jnp.concatenate([blocks[step] for step in FAR])
     wide = pltpu.VMEM((N, L), F32)

time: 134 us -> 134 us (level)
  starting transfers between devices: 22.3 us -> 25.4 us
  waiting for transfers between devices: 7.22 us -> 4.5 us
    ppermute x7, starting transfers between devices: 12.3 us -> 14.4 us  [climb(): return lax.ppermute(x, 'z', [(z, (z + step) % H) for z in range(H)])]
    ppermute x7, waiting for transfers between devices: 6.21 us -> 4.12 us  [climb(): return lax.ppermute(x, 'z', [(z, (z + step) % H) for z in range(H)])]
  transfers between devices with their start and end apart: 11 -> 11, of which waited for: 5 -> 4; matrix products, arithmetic and copies ran while one was open for 3% -> 3% of each run, Pallas kernels for 0% -> 0%
where the time goes in v2:
time: 134 us
  blocking collectives  75.4 us (56%)
  starting transfers between devices  25.4 us (19%)
  Pallas kernels  23.4 us (17%)
  waiting for transfers between devices  4.5 us (3%)
  local copies, waits for them, and re-layouts  3.51 us (3%)
    all_to_all x6, blocking collectives, share(): lax.all_to_all(jnp.broadcast_to(x[None], (B,) + x.shape), axes, 0, 0, til...  71.2 us
    pallas_call x6, Pallas kernels, call(): pl.pallas_call(kernel, out_shape=[pltpu.VMEM(x, F32) if isinstance(x, tup...  23.4 us
    ppermute x7, starting transfers between devices, climb(): return lax.ppermute(x, 'z', [(z, (z + step) % H) for z in range(H)])  14.4 us
    all_to_all x1, starting transfers between devices, share(): lax.all_to_all(jnp.broadcast_to(x[None], (B,) + x.shape), axes, 0, 0, til...  6.75 us
    ppermute x3, starting transfers between devices, swap(): return lax.ppermute(x, 'c', [(0, 1), (1, 0)])  4.23 us
    all_gather x1, blocking collectives, local(): g = lax.all_gather(g, 'c').transpose(1, 0, 2).reshape(2 * N)  4.2 us
    ppermute x7, waiting for transfers between devices, climb(): return lax.ppermute(x, 'z', [(z, (z + step) % H) for z in range(H)])  4.12 us
  transfers between devices with their start and end apart: 11, of which 4 were waited for; matrix products, arithmetic and copies ran while one was open for 3% of the time, Pallas kernels for 0%

profile of v2, /device:TPU:1, one launch (start us, length us, event | category | flops | bytes accessed | tf_op | source)
XLA Modules:
  0.0 133.8 jit_solution(1176490348368822863)
XLA Ops:
  0.6 0.0 copy-start
  0.6 2.5 %collective-permute-start = (f32[128,128]{1,0:T(8,128)}, f32[128,128]{1,0:T(8,128)S(1)}, u32[]{:S(2)}, u32[]{:S(2)}) collective-permute-start(f32[128,128]{1,0:T(8,128)} %param.4), channel_id=1, source_target_pairs={{0,1},{1,2},{2,3},{3,4},{4,5},{5,6},{6,7},{7,0},{8,9},{9,10},{10,1... | collective-permute-start | bytes 196616 | tf_op jit(solution)/shard_map/ppermute | solution.py:228
  3.2 4.0 %collective-permute-start.1 = (f32[128,128]{1,0:T(8,128)}, f32[128,128]{1,0:T(8,128)S(1)}, u32[]{:S(2)}, u32[]{:S(2)}) collective-permute-start(f32[128,128]{1,0:T(8,128)} %param.4), channel_id=1, source_target_pairs={{0,7},{1,0},{2,1},{3,2},{4,3},{5,4},{6,5},{7,6},{8,15},{9,8},{10,9... | collective-permute-start | bytes 196616 | tf_op jit(solution)/shard_map/ppermute | solution.py:228
  7.2 1.0 collective-permute-start.9
  8.2 1.9 %broadcast_in_dim.14 = f32[16,128,128]{2,1,0:T(8,128)} broadcast(f32[128,128]{1,0:T(8,128)} %param.5), dimensions={1,2} | broadcast | bytes 1114112 | tf_op jit(solution)/shard_map/broadcast_in_dim | solution.py:212
  10.1 6.8 %all-to-all-start = ((f32[16,128,128]{2,1,0:T(8,128)}), f32[16,128,128]{2,1,0:T(8,128)S(1)}, u32[]{:S(2)}, u32[]{:S(2)}) async-start(f32[16,128,128]{2,1,0:T(8,128)} %broadcast_in_dim.14), calls=%async_computation | async-start | bytes 2097152 | tf_op jit(solution)/shard_map/all_to_all | solution.py:212
  16.9 0.0 collective-permute-done
  16.9 0.1 collective-permute-start.2
  17.0 0.0 collective-permute-done.1
  17.0 2.7 %collective-permute-start.3 = (f32[128,128]{1,0:T(8,128)S(1)}, f32[128,128]{1,0:T(8,128)S(1)}, u32[]{:S(2)}, u32[]{:S(2)}) collective-permute-start(f32[128,128]{1,0:T(8,128)S(1)} %collective-permute-done.1), channel_id=1, source_target_pairs={{0,7},{1,0},{2,1},{3,2},{4,3},{5,4},{6,5},{7,6},{8,15},{9,8},{10,9... | collective-permute-start | bytes 196616 | tf_op jit(solution)/shard_map/ppermute | solution.py:228
  19.7 1.6 %collective-permute-done.2 = f32[128,128]{1,0:T(8,128)S(1)} collective-permute-done((f32[128,128]{1,0:T(8,128)S(1)}, f32[128,128]{1,0:T(8,128)S(1)}, u32[]{:S(2)}, u32[]{:S(2)}) %collective-permute-start.2) | collective-permute-done | bytes 65568 | tf_op jit(solution)/shard_map/ppermute | solution.py:228
  21.3 0.0 collective-permute-done.3
  21.3 1.5 %collective-permute-start.4 = (f32[512,128]{1,0:T(8,128)S(1)}, f32[512,128]{1,0:T(8,128)S(1)}, u32[]{:S(2)}, u32[]{:S(2)}) collective-permute-start(f32[512,128]{1,0:T(8,128)S(1)} %constant_dynamic-update-slice_fusion.near_ref), channel_id=1, source_target_pairs={{0,8},{8,0},{1,9},{9,1},{2,10},{10,2},{3,11},{11,3},{4,12},{12,4},... | collective-permute-start | bytes 786440 | tf_op jit(solution)/shard_map/ppermute | solution.py:224
  22.8 2.1 %collective-permute-start.7 = (f32[128,128]{1,0:T(8,128)S(1)}, f32[128,128]{1,0:T(8,128)S(1)}, u32[]{:S(2)}, u32[]{:S(2)}) collective-permute-start(f32[128,128]{1,0:T(8,128)S(1)} %collective-permute-done.2), channel_id=1, source_target_pairs={{0,2},{1,3},{2,4},{3,5},{4,6},{5,7},{6,0},{7,1},{8,10},{9,11},{10,... | collective-permute-start | bytes 196616 | tf_op jit(solution)/shard_map/ppermute | solution.py:228
  24.9 3.0 %collective-permute-start.5 = (f32[128,128]{1,0:T(8,128)S(1)}, f32[128,128]{1,0:T(8,128)S(1)}, u32[]{:S(2)}, u32[]{:S(2)}) collective-permute-start(f32[128,128]{1,0:T(8,128)S(1)} %collective-permute-done.2), channel_id=1, source_target_pairs={{0,1},{1,2},{2,3},{3,4},{4,5},{5,6},{6,7},{7,0},{8,9},{9,10},{10,1... | collective-permute-start | bytes 196616 | tf_op jit(solution)/shard_map/ppermute | solution.py:228
  27.9 0.0 collective-permute-start.6
  27.9 0.8 constant_dynamic-update-slice_fusion.7
  28.7 2.2 %collective-permute-done.5 = f32[128,128]{1,0:T(8,128)S(1)} collective-permute-done((f32[128,128]{1,0:T(8,128)S(1)}, f32[128,128]{1,0:T(8,128)S(1)}, u32[]{:S(2)}, u32[]{:S(2)}) %collective-permute-start.5) | collective-permute-done | bytes 65568 | tf_op jit(solution)/shard_map/ppermute | solution.py:228
  31.0 0.3 collective-permute-done.6
  31.3 0.0 collective-permute-done.7
  31.3 1.8 %collective-permute-start.8 = (f32[512,128]{1,0:T(8,128)S(1)}, f32[512,128]{1,0:T(8,128)S(1)}, u32[]{:S(2)}, u32[]{:S(2)}) collective-permute-start(f32[512,128]{1,0:T(8,128)S(1)} %constant_dynamic-update-slice_fusion.4.far_ref), channel_id=1, source_target_pairs={{0,8},{8,0},{1,9},{9,1},{2,10},{10,2},{3,11},{11,3},{4,12},{12,4},... | collective-permute-start | bytes 786440 | tf_op jit(solution)/shard_map/ppermute | solution.py:224
  33.1 0.0 copy-done
  33.1 0.7 pad_maximum_fusion.mass_ref
  33.8 0.1 pad_add_fusion.place_ref
  33.8 0.0 collective-permute-done.9.ls_other_ref
  33.9 0.0 collective-permute-done.4.near_other_ref
  33.9 0.4 collective-permute-done.8.far_other_ref
  34.2 0.0 all-to-all-done
  34.2 10.5 %start_kernel.1 = (f32[2048,2048]{1,0:T(8,128)S(1)}, f32[16,128]{1,0:T(8,128)S(1)}, f32[8,128]{1,0:T(8,128)S(1)}, f32[16,128]{1,0:T(8,128)S(1)}) custom-call(s32[2]{0:T(128)S(1)} %pad_add_fusion.place_ref, f32[512,128]{1,0:T(8,128)S(1)} %constant_dynamic-update-slice_fusion.near_ref, f32[512,128]{1,0:T(8,128)S(1)} %collective-permute-done.4.near_other_ref, ...), custom_call_target="tpu_custom_call" | custom-call | tf_op jit(solution)/shard_map/start_kernel/pallas_call | solution.py:199
  44.8 14.2 %all_to_all.35.got_ref = f32[16,16,128]{2,1,0:T(8,128)S(1)} all-to-all(f32[16,16,128]{2,1,0:T(8,128)S(1)} %broadcast_in_dim.15), channel_id=1, replica_groups=mesh['x'=4,'y'=4,'c'=2,'z'=8] {'c','z'}, dimensions={0} | all-to-all | bytes 262144 | tf_op jit(solution)/shard_map/all_to_all | solution.py:212
  59.0 6.0 %cols_kernel.1 = (f32[2048,2048]{1,0:T(8,128)S(1)}, f32[16,128]{1,0:T(8,128)S(1)}, f32[16,128]{1,0:T(8,128)S(1)}, f32[16,128]{1,0:T(8,128)S(1)}) custom-call(f32[2048,2048]{1,0:T(8,128)S(1)} %get-tuple-element.19.z_ref, f32[16,16,128]{2,1,0:T(8,128)S(1)} %all_to_all.35.got_ref, f32[16,128]{1,0:T(8,128)S(1)} %get-tuple-element.21.ls_ref), custom_call_target="tpu_custom_call", output_to_operand_aliasing={{0}: (0, {})} | custom-call | tf_op jit(solution)/shard_map/cols_kernel/pallas_call | solution.py:199
  65.1 11.3 %all_to_all.36.got_ref = f32[16,16,128]{2,1,0:T(8,128)S(1)} all-to-all(f32[16,16,128]{2,1,0:T(8,128)S(1)} %broadcast_in_dim.16), channel_id=1, replica_groups=mesh['x'=4,'y'=4,'c'=2,'z'=8] {'x','y'}, dimensions={0} | all-to-all | bytes 262144 | tf_op jit(solution)/shard_map/all_to_all | solution.py:212
  76.4 1.4 %first_row_kernel.1 = (f32[16,128]{1,0:T(8,128)S(1)}, f32[16,128]{1,0:T(8,128)S(1)}, f32[16,128]{1,0:T(8,128)S(1)}) custom-call(f32[2048,2048]{1,0:T(8,128)S(1)} %get-tuple-element.22.e_ref, f32[16,16,128]{2,1,0:T(8,128)S(1)} %all_to_all.36.got_ref, f32[16,128]{1,0:T(8,128)S(1)} %get-tuple-element.24.m_ref, f32[16,128]{1,0:T(8,128)S(1)} %bitcast.14), custom_call_target="tpu_custom_call" | custom-call | tf_op jit(solution)/shard_map/first_row_kernel/pallas_call | solution.py:199
  77.7 13.0 %all_to_all.37.got_ref = f32[16,16,128]{2,1,0:T(8,128)S(1)} all-to-all(f32[16,16,128]{2,1,0:T(8,128)S(1)} %broadcast_in_dim.17), channel_id=1, replica_groups=mesh['x'=4,'y'=4,'c'=2,'z'=8] {'c','z'}, dimensions={0} | all-to-all | bytes 262144 | tf_op jit(solution)/shard_map/all_to_all | solution.py:212
  90.8 1.8 %col_kernel.1 = f32[16,128]{1,0:T(8,128)S(1)} custom-call(f32[2048,2048]{1,0:T(8,128)S(1)} %get-tuple-element.22.e_ref, f32[16,16,128]{2,1,0:T(8,128)S(1)} %all_to_all.37.got_ref, f32[16,128]{1,0:T(8,128)S(1)} %get-tuple-element.21.ls_ref, f32[16,128]{1,0:T(8,128)S(1)} %get-tuple-element.26.v0_ref), custom_call_target="tpu_custom_call" | custom-call | tf_op jit(solution)/shard_map/col_kernel/pallas_call | solution.py:199
  92.6 9.8 %all_to_all.38.got_ref = f32[16,16,128]{2,1,0:T(8,128)S(1)} all-to-all(f32[16,16,128]{2,1,0:T(8,128)S(1)} %broadcast_in_dim.18), channel_id=1, replica_groups=mesh['x'=4,'y'=4,'c'=2,'z'=8] {'x','y'}, dimensions={0} | all-to-all | bytes 262144 | tf_op jit(solution)/shard_map/all_to_all | solution.py:212
  102.4 1.4 %row_kernel.1 = f32[16,128]{1,0:T(8,128)S(1)} custom-call(f32[2048,2048]{1,0:T(8,128)S(1)} %get-tuple-element.22.e_ref, f32[16,16,128]{2,1,0:T(8,128)S(1)} %all_to_all.38.got_ref, f32[16,128]{1,0:T(8,128)S(1)} %bitcast.15, f32[16,128]{1,0:T(8,128)S(1)} %get-tuple-element.26.v0_ref), custom_call_target="tpu_custom_call" | custom-call | tf_op jit(solution)/shard_map/row_kernel/pallas_call | solution.py:199
  103.8 13.0 %all_to_all.39.got_ref = f32[16,16,128]{2,1,0:T(8,128)S(1)} all-to-all(f32[16,16,128]{2,1,0:T(8,128)S(1)} %broadcast_in_dim.19), channel_id=1, replica_groups=mesh['x'=4,'y'=4,'c'=2,'z'=8] {'c','z'}, dimensions={0} | all-to-all | bytes 262144 | tf_op jit(solution)/shard_map/all_to_all | solution.py:212
  116.8 2.3 %last_kernel.1 = (f32[16,128]{1,0:T(8,128)S(1)}, f32[8,128]{1,0:T(8,128)}) custom-call(s32[2]{0:T(128)S(1)} %pad_add_fusion.place_ref, f32[2048,2048]{1,0:T(8,128)S(1)} %get-tuple-element.22.e_ref, f32[16,16,128]{2,1,0:T(8,128)S(1)} %all_to_all.39.got_ref, f32[16,128]{1,0:T(8,128)S(1)} %get-tuple-element.21.ls_ref, f32[16,128]{1,0:T(8,128)S(1)} %get-tuple-element.26.v0_ref, ...), custom_call_target="tpu_custom_call" | custom-call | tf_op jit(solution)/shard_map/last_kernel/pallas_call | solution.py:199
  119.1 9.8 %all_to_all.40 = f32[16,16,128]{2,1,0:T(8,128)S(1)} all-to-all(f32[16,16,128]{2,1,0:T(8,128)S(1)} %broadcast_in_dim.20), channel_id=1, replica_groups=mesh['x'=4,'y'=4,'c'=2,'z'=8] {'x','y'}, dimensions={0} | all-to-all | bytes 262144 | tf_op jit(solution)/shard_map/all_to_all | solution.py:212
  129.0 4.2 %all-gather = f32[32,128]{1,0:T(8,128)S(1)} all-gather(f32[16,128]{1,0:T(8,128)S(1)} %subtract_multiply_fusion), channel_id=2, replica_groups=mesh['x'=4,'y'=4,'c'=2,'z'=8] {'c'}, dimensions={0}, use_global_device_ids=true | all-gather | bytes 24576 | tf_op jit(solution)/shard_map/all_gather | solution.py:260
  133.2 0.6 copy.8
  (16 shorter events, 0.2 us)
Async XLA Ops:
  0.6 32.4 %copy-start = (f32[4096]{0:T(1024)S(1)}, f32[4096]{0:T(1024)}, u32[]{:S(2)}) copy-start(f32[4096]{0:T(1024)} %param.7) | copy-start | bytes 49156
  0.6 16.2 %collective-permute-start = (f32[128,128]{1,0:T(8,128)}, f32[128,128]{1,0:T(8,128)S(1)}, u32[]{:S(2)}, u32[]{:S(2)}) collective-permute-start(f32[128,128]{1,0:T(8,128)} %param.4), channel_id=1, source_target_pairs={{0,1},{1,2},{2,3},{3,4},{4,5},{5,6},{6,7},{7,0},{8,9},{9,10},{10,1... | collective-permute-start | bytes 196616 | tf_op jit(solution)/shard_map/ppermute | solution.py:228
  3.2 13.8 %collective-permute-start.1 = (f32[128,128]{1,0:T(8,128)}, f32[128,128]{1,0:T(8,128)S(1)}, u32[]{:S(2)}, u32[]{:S(2)}) collective-permute-start(f32[128,128]{1,0:T(8,128)} %param.4), channel_id=1, source_target_pairs={{0,7},{1,0},{2,1},{3,2},{4,3},{5,4},{6,5},{7,6},{8,15},{9,8},{10,9... | collective-permute-start | bytes 196616 | tf_op jit(solution)/shard_map/ppermute | solution.py:228
  7.2 26.6 %collective-permute-start.9 = (f32[8,128]{1,0:T(8,128)}, f32[8,128]{1,0:T(8,128)S(1)}, u32[]{:S(2)}, u32[]{:S(2)}) collective-permute-start(f32[8,128]{1,0:T(8,128)} %bitcast.19), channel_id=1, source_target_pairs={{0,8},{8,0},{1,9},{9,1},{2,10},{10,2},{3,11},{11,3},{4,12},{12,4},... | collective-permute-start | bytes 12296 | tf_op jit(solution)/shard_map/ppermute | solution.py:224
  10.1 24.1 %all-to-all-start = ((f32[16,128,128]{2,1,0:T(8,128)}), f32[16,128,128]{2,1,0:T(8,128)S(1)}, u32[]{:S(2)}, u32[]{:S(2)}) async-start(f32[16,128,128]{2,1,0:T(8,128)} %broadcast_in_dim.14), calls=%async_computation | async-start | bytes 2097152 | tf_op jit(solution)/shard_map/all_to_all | solution.py:212
  16.9 4.4 %collective-permute-start.2 = (f32[128,128]{1,0:T(8,128)S(1)}, f32[128,128]{1,0:T(8,128)S(1)}, u32[]{:S(2)}, u32[]{:S(2)}) collective-permute-start(f32[128,128]{1,0:T(8,128)S(1)} %collective-permute-done), channel_id=1, source_target_pairs={{0,1},{1,2},{2,3},{3,4},{4,5},{5,6},{6,7},{7,0},{8,9},{9,10},{10,1... | collective-permute-start | bytes 196616 | tf_op jit(solution)/shard_map/ppermute | solution.py:228
  17.0 4.3 %collective-permute-start.3 = (f32[128,128]{1,0:T(8,128)S(1)}, f32[128,128]{1,0:T(8,128)S(1)}, u32[]{:S(2)}, u32[]{:S(2)}) collective-permute-start(f32[128,128]{1,0:T(8,128)S(1)} %collective-permute-done.1), channel_id=1, source_target_pairs={{0,7},{1,0},{2,1},{3,2},{4,3},{5,4},{6,5},{7,6},{8,15},{9,8},{10,9... | collective-permute-start | bytes 196616 | tf_op jit(solution)/shard_map/ppermute | solution.py:228
  21.3 12.5 %collective-permute-start.4 = (f32[512,128]{1,0:T(8,128)S(1)}, f32[512,128]{1,0:T(8,128)S(1)}, u32[]{:S(2)}, u32[]{:S(2)}) collective-permute-start(f32[512,128]{1,0:T(8,128)S(1)} %constant_dynamic-update-slice_fusion.near_ref), channel_id=1, source_target_pairs={{0,8},{8,0},{1,9},{9,1},{2,10},{10,2},{3,11},{11,3},{4,12},{12,4},... | collective-permute-start | bytes 786440 | tf_op jit(solution)/shard_map/ppermute | solution.py:224
  22.8 8.5 %collective-permute-start.7 = (f32[128,128]{1,0:T(8,128)S(1)}, f32[128,128]{1,0:T(8,128)S(1)}, u32[]{:S(2)}, u32[]{:S(2)}) collective-permute-start(f32[128,128]{1,0:T(8,128)S(1)} %collective-permute-done.2), channel_id=1, source_target_pairs={{0,2},{1,3},{2,4},{3,5},{4,6},{5,7},{6,0},{7,1},{8,10},{9,11},{10,... | collective-permute-start | bytes 196616 | tf_op jit(solution)/shard_map/ppermute | solution.py:228
  24.9 6.0 %collective-permute-start.5 = (f32[128,128]{1,0:T(8,128)S(1)}, f32[128,128]{1,0:T(8,128)S(1)}, u32[]{:S(2)}, u32[]{:S(2)}) collective-permute-start(f32[128,128]{1,0:T(8,128)S(1)} %collective-permute-done.2), channel_id=1, source_target_pairs={{0,1},{1,2},{2,3},{3,4},{4,5},{5,6},{6,7},{7,0},{8,9},{9,10},{10,1... | collective-permute-start | bytes 196616 | tf_op jit(solution)/shard_map/ppermute | solution.py:228
  27.9 3.4 %collective-permute-start.6 = (f32[128,128]{1,0:T(8,128)S(1)}, f32[128,128]{1,0:T(8,128)S(1)}, u32[]{:S(2)}, u32[]{:S(2)}) collective-permute-start(f32[128,128]{1,0:T(8,128)S(1)} %collective-permute-done.3), channel_id=1, source_target_pairs={{0,7},{1,0},{2,1},{3,2},{4,3},{5,4},{6,5},{7,6},{8,15},{9,8},{10,9... | collective-permute-start | bytes 196616 | tf_op jit(solution)/shard_map/ppermute | solution.py:228
  31.3 2.9 %collective-permute-start.8 = (f32[512,128]{1,0:T(8,128)S(1)}, f32[512,128]{1,0:T(8,128)S(1)}, u32[]{:S(2)}, u32[]{:S(2)}) collective-permute-start(f32[512,128]{1,0:T(8,128)S(1)} %constant_dynamic-update-slice_fusion.4.far_ref), channel_id=1, source_target_pairs={{0,8},{8,0},{1,9},{9,1},{2,10},{10,2},{3,11},{11,3},{4,12},{12,4},... | collective-permute-start | bytes 786440 | tf_op jit(solution)/shard_map/ppermute | solution.py:224
